TPU v7x, 32 devices: a whole 2x2x4 slice. The times are simulated.
32 devices in a mesh: dp: 8 (over z, core), bal: 4 (over y, x).
Axes of the slice: x: 2, y: 2, z: 4, core: 2. Of those that a mesh axis runs over, the one named last changes fastest.
Arguments:
- tiles: bfloat16 [736, 270, 256], P(('dp', 'bal')), may hold values from -6 to 6
- cotangent: bfloat16 [736, 32, 256], P(('dp', 'bal')), may hold values from -6 to 6
- halo_flags: int32 [736, 3], P(('dp', 'bal')), may hold values 0 or 1
- send_plan: int32 [32, 4, 6], P(('dp', 'bal')), may hold values from -1 to 22, as said below
- spatial_weight: bfloat16 [2304, 256], P('bal'), may hold values from -0.125 to 0.125
- temporal_weight: bfloat16 [512, 256], P('bal'), may hold values from -0.25 to 0.25
Outputs:
- features: bfloat16 [736, 32, 256], P(('dp', 'bal'))
- spatial_grad: float32 [2304, 256], P('bal', 'dp')
- temporal_grad: float32 [512, 256], P('bal', 'dp')
Inputs may be any that keep to these rules, and one draw needn't show every extreme that they name: `send_plan`: row g lists, for each worker w of owner g's bal group (bal index w, same dp index) and each pair slot q, the owner's tile slot sent there, or -1. The live slots of an owner are its slots 0 to n - 1, each named exactly once, with n from 1 to 23; in every group some owner has exactly 23. One owner sends at most 6 tiles to one worker, and some pair holds exactly 6; every worker receives exactly 12 tiles.
All inputs are finite; a program needn't handle non-finite values. No bound on the sum of `halo_flags` on one device may be relied on, other than what follows from the above.
Results may differ from a plain program's by a relative error of at most 0.0049.
Values may be sent and summed in bfloat16 or wider, within the bound.
A program may use at most 128 MiB of HBM per device.

v0:
```python
import math

import jax
import jax.numpy as jnp
from jax import lax
from jax.sharding import PartitionSpec as P

TILE_ROWS = 2
TILE_COLUMNS = 4
OUTPUT_FRAMES = 4
TEMPORAL_DILATION = 2
WORK_TILES = 12
IN_FR = 6
IN_H = 5
IN_W = 9
OUT_PIX = 32


def keep_mask(halo_flag_row):
    frame_indices = jnp.arange(IN_FR)[:, None, None]
    row_ids = jnp.arange(IN_H)[None, :, None]
    col_ids = jnp.arange(IN_W)[None, None, :]
    top_ok = (row_ids > 0) | (halo_flag_row[0] > 0)
    left_ok = (col_ids > 0) | (halo_flag_row[1] > 0)
    past_frame_valid = (frame_indices >= TEMPORAL_DILATION) | (halo_flag_row[2] > 0)
    return top_ok & left_ok & past_frame_valid


def tile_pass(inputs, cotang, spatial_full, temporal_full):
    tile_number = inputs.shape[0]
    channel_index = inputs.shape[-1]
    tap_list = []
    for row_tap in range(3):
        for col_tap in range(3):
            tap_list.append(
                inputs[
                    :,
                    :,
                    row_tap : row_tap + 2 * TILE_ROWS - 1 : 2,
                    col_tap : col_tap + 2 * TILE_COLUMNS - 1 : 2,
                    :,
                ]
            )
    patches = jnp.concatenate(tap_list, axis=-1).reshape(-1, 9 * channel_index)
    pre_act = jnp.dot(patches, spatial_full, preferred_element_type=jnp.float32)
    activation = (
        jax.nn.silu(pre_act)
        .astype(jnp.bfloat16)
        .reshape(tile_number, IN_FR, TILE_ROWS * TILE_COLUMNS, channel_index)
    )
    paired_tiles = jnp.concatenate(
        [activation[:, TEMPORAL_DILATION:], activation[:, :OUTPUT_FRAMES]], axis=-1
    ).reshape(-1, 2 * channel_index)
    outputs = jnp.dot(paired_tiles, temporal_full, preferred_element_type=jnp.float32).astype(
        jnp.bfloat16
    )
    grad_out = cotang.reshape(-1, channel_index)
    grad_temp = lax.dot_general(
        paired_tiles, grad_out, (((0,), (0,)), ((), ())), preferred_element_type=jnp.float32
    )
    grad_pair = lax.dot_general(
        grad_out, temporal_full, (((1,), (1,)), ((), ())), preferred_element_type=jnp.float32
    )
    grad_pair = grad_pair.reshape(
        tile_number, OUTPUT_FRAMES, TILE_ROWS * TILE_COLUMNS, 2 * channel_index
    )
    causal_padding = jnp.zeros(
        (tile_number, TEMPORAL_DILATION, TILE_ROWS * TILE_COLUMNS, channel_index), jnp.float32
    )
    grad_activ = jnp.concatenate(
        [causal_padding, grad_pair[..., :channel_index]], axis=1
    ) + jnp.concatenate([grad_pair[..., channel_index:], causal_padding], axis=1)
    pre_view = pre_act.reshape(grad_activ.shape)
    sigmoid_v = jax.nn.sigmoid(pre_view)
    grad_pre = (
        (grad_activ * sigmoid_v * (1.0 + pre_view * (1.0 - sigmoid_v)))
        .astype(jnp.bfloat16)
        .reshape(-1, channel_index)
    )
    grad_space = lax.dot_general(
        patches, grad_pre, (((0,), (0,)), ((), ())), preferred_element_type=jnp.float32
    )
    return (outputs.reshape(tile_number, OUT_PIX, channel_index), grad_space, grad_temp)


def per_device(tiles, cotangent, halo_flags, send_plan, spatial_weight, temporal_weight):
    owned = tiles.shape[0]
    channel_index = tiles.shape[-1]
    spatial_full, temporal_full = (
        lax.all_gather(spatial_weight, "bal", axis=0, tiled=True),
        lax.all_gather(temporal_weight, "bal", axis=0, tiled=True),
    )
    shaped = tiles.reshape(owned, IN_FR, IN_H, IN_W, channel_index)
    keeping = jax.vmap(keep_mask)(halo_flags)
    masked = jnp.where(keeping[..., None], shaped, jnp.zeros_like(shaped))
    route_rows = send_plan[0]
    live_slots = jnp.any(
        route_rows.reshape(-1)[:, None] == jnp.arange(owned, dtype=jnp.int32)[None, :], axis=0
    )
    live_cot = jnp.where(live_slots[:, None, None], cotangent, jnp.zeros((), jnp.bfloat16))
    outputs, grad_space, grad_temp = tile_pass(
        masked,
        live_cot.reshape(owned, OUTPUT_FRAMES, TILE_ROWS, TILE_COLUMNS, channel_index),
        spatial_full,
        temporal_full,
    )
    features = jnp.where(live_slots[:, None, None], outputs, jnp.zeros((), jnp.bfloat16))
    data_count = lax.axis_size("dp")
    group_size = lax.axis_size("bal")
    factor = 1.0 / math.sqrt(data_count * group_size * WORK_TILES)
    part_space, part_temp = (
        lax.psum_scatter(grad_space, "dp", scatter_dimension=1, tiled=True),
        lax.psum_scatter(grad_temp, "dp", scatter_dimension=1, tiled=True),
    )
    sum_space, sum_temp = (
        lax.psum_scatter(part_space, "bal", scatter_dimension=0, tiled=True),
        lax.psum_scatter(part_temp, "bal", scatter_dimension=0, tiled=True),
    )
    return (features, sum_space * factor, sum_temp * factor)


def solution(mesh):
    in_specs = (
        P(("dp", "bal"), None, None),
        P(("dp", "bal"), None, None),
        P(("dp", "bal"), None),
        P(("dp", "bal"), None, None),
        P("bal", None),
        P("bal", None),
    )
    out_specs = (P(("dp", "bal"), None, None), P("bal", "dp"), P("bal", "dp"))
    return jax.shard_map(
        per_device, mesh=mesh, in_specs=in_specs, out_specs=out_specs, check_vma=False
    )
```

profile of v0, /device:TPU:0, one launch (start us, length us, event | category | flops | bytes accessed | tf_op | source)
XLA Modules:
  0.0 183.5 jit_solution(4347617537107884745)
XLA Ops:
  7.2 0.0 all-gather.2.cloned.1.call-start
  7.2 0.7 all-gather.2.cloned.1.call-update
  7.9 0.0 reduce-scatter.9.cloned.1.call-start
  8.0 0.8 compare_bitcast_fusion.2
  8.8 3.0 %copy.14 = bf16[23,270,256]{2,0,1:T(8,128)(2,1)S(1)} copy(bf16[23,270,256]{2,1,0:T(8,128)(2,1)} %param.6) | data formatting | bytes 6359040 | tf_op args[0]
  11.8 0.1 broadcast_or_fusion
  11.9 0.1 broadcast_or_fusion.2
  12.0 0.1 broadcast_or_fusion.1
  12.1 1.3 broadcast_select_fusion
  13.4 0.1 slice_dynamic-update-slice_fusion.8
  13.4 0.1 slice_dynamic-update-slice_fusion.7
  13.5 0.1 slice_dynamic-update-slice_fusion.6
  13.5 0.1 slice_dynamic-update-slice_fusion.5
  13.6 0.1 slice_dynamic-update-slice_fusion.4
  13.7 0.1 slice_dynamic-update-slice_fusion.3
  13.7 0.1 slice_dynamic-update-slice_fusion.2
  13.8 0.1 slice_dynamic-update-slice_fusion.1
  13.8 0.1 slice_dynamic-update-slice_fusion
  13.9 4.3 %copy.15 = bf16[23,6,2,4,2304]{4,3,2,1,0:T(4,128)(2,1)} copy(bf16[23,6,2,4,2304]{4,0,3,2,1:T(8,128)(2,1)S(1)} %slice_dynamic-update-slice_fusion) | data formatting | bytes 10174464 | tf_op jit(solution)/shard_map/concatenate | solution.py:44
  18.2 0.0 copy-start.2
  18.2 0.0 copy-start.1
  18.2 8.9 %reshape.174 = bf16[1104,2304]{1,0:T(8,128)(2,1)} reshape(bf16[23,6,2,4,2304]{4,3,2,1,0:T(4,128)(2,1)} %copy.15) | data formatting | bytes 10174464 | tf_op jit(solution)/shard_map/reshape | solution.py:44
  27.1 0.0 copy-done.2
  27.1 0.1 eq.15
  27.2 0.0 copy-done.1
  27.2 12.4 %all_gather.7 = bf16[512,256]{1,0:T(8,128)(2,1)S(1)} all-gather(bf16[128,256]{1,0:T(8,128)(2,1)S(1)} %copy-done.1), channel_id=1, replica_groups=mesh['dp'=8,'bal'=4] {'bal'}, dimensions={0}, use_global_device_ids=true | all-gather | bytes 327680 | tf_op jit(solution)/shard_map/all_gather | solution.py:91
  39.6 0.1 fusion.3
  39.7 2.4 %all-gather.2.cloned.1.call-done = bf16[2304,256]{1,0:T(8,128)(2,1)} async-done(((bf16[576,256]{1,0:T(8,128)(2,1)}), bf16[2304,256]{1,0:T(8,128)(2,1)}) %all-gather.2.cloned.1.call-update) | async-done | bytes 1179664 | tf_op jit(solution)/shard_map/all_gather | solution.py:90
  42.1 4.3 %multiply_convert_fusion.1 = (bf16[1104,256]{1,0:T(8,128)(2,1)S(1)}, f32[1104,256]{1,0:T(8,128)S(1)}) fusion(bf16[1104,2304]{1,0:T(8,128)(2,1)} %reshape.174, bf16[2304,256]{1,0:T(8,128)(2,1)} %all-gather.2.cloned.1.call-done), kind=kOutput, calls=%fused_computation.3 | convolution fusion | flops 1303744512 | bytes 7962624 | tf_op jit(solution)/shard_map/dot_general | solution.py:45
  46.4 0.0 copy-start
  46.4 0.1 fusion.5
  46.5 0.1 pad_maximum_fusion
  46.5 0.4 convolution_convert_fusion
  46.9 0.5 copy-done
  47.4 0.9 broadcast_select_fusion.1
  48.2 0.4 fusion
  48.6 1.2 fusion.7
  49.9 0.0 reduce-scatter.9.cloned.1.call-update
  49.9 0.0 reduce-scatter.7.cloned.1.call-start
  49.9 0.2 fusion.4
  50.1 0.5 multiply_convert_fusion
  50.6 5.6 %fusion.6 = f32[2304,256]{0,1:T(8,128)} fusion(bf16[1104,2304]{1,0:T(8,128)(2,1)} %reshape.174, bf16[1104,256]{1,0:T(8,128)(2,1)S(1)} %bitcast.37), kind=kOutput, calls=%fused_computation.36 | convolution fusion | flops 1302331392 | bytes 8011776 | tf_op jit(solution)/shard_map/dot_general | solution.py:80
  56.3 0.0 reduce-scatter.7.cloned.1.call-update
  56.3 0.0 reduce-scatter.11.cloned.1.call-start
  56.3 24.9 %reduce-scatter.9.cloned.1.call-done = f32[512,32]{0,1:T(8,128)} async-done(((f32[512,256]{0,1:T(8,128)}), f32[512,32]{0,1:T(8,128)}) %reduce-scatter.9.cloned.1.call-update) | async-done | bytes 65552 | tf_op jit(solution)/shard_map/reduce_scatter | solution.py:113
  81.3 0.0 reduce-scatter.11.cloned.1.call-update
  81.3 0.0 reduce-scatter.13.cloned.1.call-start
  81.3 36.8 %reduce-scatter.7.cloned.1.call-done = f32[2304,32]{0,1:T(8,128)} async-done(((f32[2304,256]{0,1:T(8,128)}), f32[2304,32]{0,1:T(8,128)}) %reduce-scatter.7.cloned.1.call-update) | async-done | bytes 294928 | tf_op jit(solution)/shard_map/reduce_scatter | solution.py:112
  118.1 2.4 %copy.17 = f32[2304,32]{1,0:T(8,128)} copy(f32[2304,32]{0,1:T(8,128)} %reduce-scatter.7.cloned.1.call-done) | data formatting | bytes 589824
  120.5 0.0 reduce-scatter.13.cloned.1.call-update
  120.5 23.3 %reduce-scatter.11.cloned.1.call-done = f32[128,32]{0,1:T(8,128)} async-done(((f32[512,32]{0,1:T(8,128)}), f32[128,32]{0,1:T(8,128)}) %reduce-scatter.11.cloned.1.call-update) | async-done | bytes 16400 | tf_op jit(solution)/shard_map/reduce_scatter | solution.py:117
  143.8 1.3 broadcast_multiply_fusion.1
  145.2 30.0 %reduce-scatter.13.cloned.1.call-done = f32[576,32]{1,0:T(8,128)} async-done(((f32[2304,32]{1,0:T(8,128)}), f32[576,32]{1,0:T(8,128)}) %reduce-scatter.13.cloned.1.call-update) | async-done | bytes 73744
  175.2 1.1 copy.18
  176.3 0.7 broadcast_multiply_fusion
  (5 shorter events, 0.1 us)
Async XLA Ops:
  7.2 34.9 %all-gather.2.cloned.1.call-start = ((), (), s32[]{:S(2)}) async-start(), calls=%async_computation.4 | async-start | bytes 1474560 | tf_op jit(solution)/shard_map/all_gather | solution.py:90
  7.9 73.4 %reduce-scatter.9.cloned.1.call-start = ((), (), s32[]{:S(2)}) async-start(), calls=%async_computation.6 | async-start | bytes 589824 | tf_op jit(solution)/shard_map/reduce_scatter | solution.py:113
  18.2 8.9 %copy-start.2 = (s32[1,4,6]{2,1,0:T(4,128)S(1)}, s32[1,4,6]{2,1,0:T(4,128)}, u32[]{:S(2)}) copy-start(s32[1,4,6]{2,1,0:T(4,128)} %param.9) | copy-start | bytes 292
  18.2 9.0 %copy-start.1 = (bf16[128,256]{1,0:T(8,128)(2,1)S(1)}, bf16[128,256]{1,0:T(8,128)(2,1)}, u32[]{:S(2)}) copy-start(bf16[128,256]{1,0:T(8,128)(2,1)} %param.11) | copy-start | bytes 196612
  46.4 1.0 copy-start
  49.9 68.3 %reduce-scatter.7.cloned.1.call-start = ((), (), s32[]{:S(2)}) async-start(), calls=%async_computation.5 | async-start | bytes 2654208 | tf_op jit(solution)/shard_map/reduce_scatter | solution.py:112
  56.3 87.5 %reduce-scatter.11.cloned.1.call-start = ((), (), s32[]{:S(2)}) async-start(), calls=%async_computation.7 | async-start | bytes 81920 | tf_op jit(solution)/shard_map/reduce_scatter | solution.py:117
  81.3 93.9 %reduce-scatter.13.cloned.1.call-start = ((), (), s32[]{:S(2)}) async-start(), calls=%async_computation.8 | async-start | bytes 1474560
Sparse Core Ops, SparseCore 0:
  9.8 32.2 all-gather.1
  50.0 31.2 reduce-scatter.8
  83.7 34.4 reduce-scatter.6
  120.9 22.8 reduce-scatter.10
  146.6 28.5 reduce-scatter.12
where the time goes:
time: 184 us; the launch traced here: 183 us
  waiting for transfers between devices  118 us (64%)
  local copies, waits for them, and re-layouts  21 us (11%)
  between operations  13.9 us (8%)
  blocking collectives  12.4 us (7%)
  matrix products  11.9 us (6%)
  other arithmetic  5.83 us (3%)
    reduce_scatter x1, waiting for transfers between devices, per_device(): lax.psum_scatter(grad_space, 'dp', scatter_dimension=1, tiled=True)  36.8 us
    unnamed x6, waiting for transfers between devices  30.8 us
    reduce_scatter x1, waiting for transfers between devices, per_device(): lax.psum_scatter(grad_temp, 'dp', scatter_dimension=1, tiled=True)  24.9 us
    reduce_scatter x1, waiting for transfers between devices, per_device(): lax.psum_scatter(part_temp, 'bal', scatter_dimension=0, tiled=True)  23.3 us
    all_gather x1, blocking collectives, per_device(): lax.all_gather(temporal_weight, 'bal', axis=0, tiled=True)  12.4 us
    reshape x1, local copies, waits for them, and re-layouts, tile_pass(): patches = jnp.concatenate(tap_list, axis=-1).reshape(-1, 9 * channel_index)  8.9 us
    unnamed x17, local copies, waits for them, and re-layouts  7.41 us
    dot_general x1, matrix products, tile_pass(): lax.dot_general(patches, grad_pre, (((0,), (0,)), ((), ())), preferred_el...  5.64 us
  transfers between devices with their start and end apart: 5, of which 5 were waited for; matrix products, arithmetic and copies ran while one was open for 16% of the time, Pallas kernels for 0%

commit v1 on v0

v1 whole, which is shorter than its diff:
```python
import functools
import math

import jax
import jax.numpy as jnp
from jax import lax
from jax.experimental import pallas as pl
from jax.experimental.pallas import tpu as pltpu
from jax.sharding import PartitionSpec as P

FR, H, W = 6, 5, 9
TR, TC, TO = 2, 4, 4
WORK_TILES = 12
F32, BF16 = jnp.float32, jnp.bfloat16
MESH = pl.DeviceIdType.MESH


def up(value, step):
    return (value + step - 1) // step * step


def kernel(
    cfg,
    tiles_ref, cot_ref, flags_ref, plan_ref, wsp_ref, wtp_ref,
    feat_ref, grad_ref,
    tbuf, xf, cf, patches, cotp, wsp, wtp, act, dact, grad_t, cot_t, live, masks,
    own, s1, r1, s2, r2, own3, s3, r3,
    tile_sem, loc_sem, ag_send, ag_recv, fw_send, fw_recv,
    s1_send, s1_recv, s2_send, s2_recv, s3_send, s3_recv,
):
    nd, nb, owned, C = cfg["nd"], cfg["nb"], cfg["owned"], cfg["C"]
    S, rs, rt, nt, nl = cfg["S"], cfg["rs"], cfg["rt"], cfg["nt"], cfg["nl"]
    cw, cwp, parts = cfg["cw"], cfg["cwp"], cfg["parts"]
    nz = nd // 2
    cells, opix = FR * H * W, TO * TR * TC
    ts, cs = cells + 1, opix + 1
    FS = TR * TC * S
    half = C // 2

    d = lax.axis_index("dp")
    b = lax.axis_index("bal")
    core = lax.rem(d, 2)
    z = d // 2
    mate = d + 1 - 2 * core

    def bal_peer(k):
        return lax.rem(b + k, nb)

    def z_peer(k):
        return lax.rem(z + k, nz)

    tile_copies = []
    lo = 0
    for n, count in enumerate(parts):
        cp = pltpu.make_async_copy(
            tiles_ref.at[pl.ds(lo, count)], tbuf.at[pl.ds(lo, count)], tile_sem.at[n]
        )
        cp.start()
        tile_copies.append((cp, lo, count))
        lo += count
    my_sp = pl.ds(pl.multiple_of(b * rs, 16), rs)
    my_tp = pl.ds(pl.multiple_of(b * rt, 16), rt)
    local = [
        pltpu.make_async_copy(wsp_ref, wsp.at[my_sp], loc_sem.at[0]),
        pltpu.make_async_copy(wtp_ref, wtp.at[my_tp], loc_sem.at[1]),
    ]
    for cp in local:
        cp.start()

    barrier = pltpu.get_barrier_semaphore()
    pl.semaphore_signal(barrier, inc=1, device_id=(mate, b), device_id_type=MESH)
    for k in range(1, nb):
        pl.semaphore_signal(barrier, inc=1, device_id=(d, bal_peer(k)), device_id_type=MESH)
    for k in range(1, nz):
        pl.semaphore_signal(
            barrier, inc=1, device_id=(2 * z_peer(k) + core, b), device_id_type=MESH
        )
    pl.semaphore_wait(barrier, nb + nz - 1)

    lanes = pl.ds(pl.multiple_of(core * half, 128), half)
    gathers = []
    for k in range(1, nb):
        for n, (src, dst, rows) in enumerate(((wsp_ref, wsp, my_sp), (wtp_ref, wtp, my_tp))):
            cp = pltpu.make_async_remote_copy(
                src_ref=src.at[:, lanes],
                dst_ref=dst.at[rows, lanes],
                send_sem=ag_send.at[n, k - 1],
                recv_sem=ag_recv.at[n, k - 1],
                device_id=(d, bal_peer(k)),
                device_id_type=MESH,
            )
            cp.start()
            gathers.append(cp)

    masks[...] = jnp.zeros_like(masks)
    flags = flags_ref[...]
    for n in range(3):
        masks[n, 0:owned, :] = jnp.broadcast_to(
            (flags[:, n : n + 1] > 0).astype(F32), (owned, 128)
        )
    slot = lax.broadcasted_iota(jnp.int32, (S, 128), 0)
    found = jnp.zeros((S, 128), F32)
    for w in range(plan_ref.shape[1]):
        for q in range(plan_ref.shape[2]):
            found = jnp.maximum(found, jnp.where(slot == plan_ref[0, w, q], 1.0, 0.0))
    live[...] = found

    if S > owned:
        for h in range(2):
            cf[h, owned * cs : S * cs, :] = jnp.zeros(((S - owned) * cs, 128), F32)
            xf[h, owned * ts : S * ts, :] = jnp.zeros(((S - owned) * ts, 128), F32)

    def cot_in(s, carry):
        v = cot_ref[s].astype(F32)
        for h in range(2):
            cf[h, pl.ds(s * cs, opix), :] = v[:, h * 128 : (h + 1) * 128]
        return carry

    lax.fori_loop(0, owned, cot_in, 0)
    lv = live[...]

    def cot_rows(p, carry):
        for h in range(2):
            pair = [
                cf[h, pl.ds(2 * p + n, S, stride=cs), :] * lv for n in range(2)
            ]
            cotp[pl.ds(pl.multiple_of(p * 2 * S, 16), 2 * S), h * 128 : (h + 1) * 128] = (
                jnp.concatenate(pair, axis=0).astype(BF16)
            )
        return carry

    lax.fori_loop(0, opix // 2, cot_rows, 0)

    def tile_in(s, carry):
        v = tbuf[s].astype(F32)
        for h in range(2):
            xf[h, pl.ds(s * ts, cells), :] = v[:, h * 128 : (h + 1) * 128]
        return carry

    for cp, lo, count in tile_copies:
        cp.wait()
        lax.fori_loop(lo, lo + count, tile_in, 0)

    top, left, past = masks[0], masks[1], masks[2]

    def patch_rows(f, carry):
        hist = jnp.where(f >= 2, jnp.ones_like(past), past)
        hist_top, hist_left = hist * top, hist * left
        hist_both = hist_top * left
        for i in range(TR):
            for jp in range(TC // 2):
                row = pl.ds(pl.multiple_of(f * FS + (i * TC + 2 * jp) * S, 16), 2 * S)
                for ky in range(3):
                    for kx in range(3):
                        on_top = 2 * i + ky == 0
                        on_left = jp == 0 and kx == 0
                        first = (
                            hist_both if on_top and on_left
                            else hist_top if on_top
                            else hist_left if on_left
                            else hist
                        )
                        second = hist_top if on_top else hist
                        cell = f * (H * W) + (2 * i + ky) * W + 4 * jp + kx
                        tap = 3 * ky + kx
                        for h in range(2):
                            v0 = xf[h, pl.ds(cell, S, stride=ts), :] * first
                            v1 = xf[h, pl.ds(cell + 2, S, stride=ts), :] * second
                            patches[row, tap * C + h * 128 : tap * C + (h + 1) * 128] = (
                                jnp.concatenate([v0, v1], axis=0).astype(BF16)
                            )
        return carry

    lax.fori_loop(0, FR, patch_rows, 0)

    def split_rows(v):
        cores = [
            jnp.concatenate(
                [v[(2 * n + q) * cw : (2 * n + q + 1) * cw] for n in range(nz)], axis=0
            )
            for q in range(2)
        ]
        return cores

    def store_split(ref, v, lo, width):
        cores = split_rows(v)
        for q in range(2):
            at = core if q == 1 else 0
            at = (1 - core) if q == 1 else core
            ref[pl.ds(pl.multiple_of(at * half, 128), half), lo : lo + width] = cores[
                q
            ].astype(BF16)

    for n in range(2):
        rows = n * 2 * FS
        store_split(cot_t, cotp[rows : rows + 2 * FS, :].astype(F32).T, rows, 2 * FS)

    for cp in local:
        cp.wait()
    forwards = []
    for k in range(1, nb):
        origin = lax.rem(b + nb - k, nb)
        for n, (dst, size) in enumerate(((wsp, rs), (wtp, rt))):
            gathers[2 * (k - 1) + n].wait_recv()
            rows = pl.ds(pl.multiple_of(origin * size, 16), size)
            cp = pltpu.make_async_remote_copy(
                src_ref=dst.at[rows, lanes],
                dst_ref=dst.at[rows, lanes],
                send_sem=fw_send.at[n, k - 1],
                recv_sem=fw_recv.at[n, k - 1],
                device_id=(mate, b),
                device_id_type=MESH,
            )
            cp.start()
            forwards.append(cp)
    for cp in forwards:
        cp.wait_recv()

    def chunk(n):
        rows = n * 2 * FS
        pre = jnp.dot(patches[rows : rows + 2 * FS, :], wsp[...], preferred_element_type=F32)
        sig = 1.0 / (1.0 + jnp.exp(-pre))
        act[rows : rows + 2 * FS, :] = (pre * sig).astype(BF16)
        ga = None
        nt_dims = (((1,), (1,)), ((), ()))
        if n > 0:
            lo = (n - 1) * 2 * FS
            ga = lax.dot_general(
                cotp[lo : lo + 2 * FS, :], wtp[0:C, :], nt_dims, preferred_element_type=F32
            )
        if n < 2:
            g = lax.dot_general(
                cotp[rows : rows + 2 * FS, :], wtp[C : 2 * C, :], nt_dims,
                preferred_element_type=F32,
            )
            ga = g if ga is None else ga + g
        gp = ga * (sig * (1.0 + pre * (1.0 - sig)))
        store_split(grad_t, gp.T, rows, 2 * FS)

    for n in range(3):
        chunk(n)

    sp_lanes = nt * 128

    def section(k):
        to = bal_peer(k)
        sp_at = pl.multiple_of((to * rs) // 128 * 128, 128)
        g = jnp.dot(grad_t[...], patches[:, pl.ds(sp_at, sp_lanes)], preferred_element_type=F32)
        own[k - 1, :, 0:sp_lanes] = g[0:half]
        s1[k - 1, :, 0:sp_lanes] = g[half:].astype(BF16)
        tp_at = (to * rt) // 128 * 128
        tap = tp_at // C
        at = pl.multiple_of(tp_at - tap * C, 128)
        rows = pl.ds(pl.multiple_of((1 - tap) * 2 * FS, 16), TO * FS)
        g = jnp.dot(cot_t[...], act[rows, pl.ds(at, 128)], preferred_element_type=F32)
        own[k - 1, :, sp_lanes:] = g[0:half]
        s1[k - 1, :, sp_lanes:] = g[half:].astype(BF16)
        cp = pltpu.make_async_remote_copy(
            src_ref=s1.at[k - 1], dst_ref=r1.at[k - 1],
            send_sem=s1_send.at[k - 1], recv_sem=s1_recv.at[k - 1],
            device_id=(mate, b), device_id_type=MESH,
        )
        cp.start()
        return cp

    first = {}
    second = {}

    def pass_on(k):
        first[k].wait_recv()
        total = own[k - 1] + r1[k - 1].astype(F32)
        if k == nb:
            own[k - 1] = total
            return
        s2[k - 1] = total.astype(BF16)
        cp = pltpu.make_async_remote_copy(
            src_ref=s2.at[k - 1], dst_ref=r2.at[k - 1],
            send_sem=s2_send.at[k - 1], recv_sem=s2_recv.at[k - 1],
            device_id=(d, bal_peer(k)), device_id_type=MESH,
        )
        cp.start()
        second[k] = cp

    for k in range(1, nb + 1):
        first[k] = section(k)
        if k > 1:
            pass_on(k - 1)
    pass_on(nb)

    def features(t0):
        rows = t0 * FS
        feat = jnp.dot(
            act[rows + 2 * FS : rows + 4 * FS, :], wtp[0:C, :], preferred_element_type=F32
        ) + jnp.dot(act[rows : rows + 2 * FS, :], wtp[C : 2 * C, :], preferred_element_type=F32)
        for p in range(2 * TR * TC):
            for h in range(2):
                v = feat[p * S : (p + 1) * S, h * 128 : (h + 1) * 128]
                cf[h, pl.ds(t0 * TR * TC + p, S, stride=cs), :] = v * lv

    features(0)
    features(2)

    def feat_out(s, carry):
        feat_ref[s] = jnp.concatenate(
            [cf[h, pl.ds(s * cs, opix), :] for h in range(2)], axis=1
        ).astype(BF16)
        return carry

    lax.fori_loop(0, owned, feat_out, 0)

    total = own[nb - 1]
    for k in range(1, nb):
        second[k].wait_recv()
        total = total + r2[k - 1].astype(F32)
    for n in range(nz):
        part = total[n * cw : (n + 1) * cw]
        own3[n] = part
        if cwp > cw:
            part = jnp.concatenate([part, jnp.zeros((cwp - cw, nl), F32)], axis=0)
        s3[n] = part.astype(BF16)
    third = []
    for k in range(1, nz):
        to = z_peer(k)
        cp = pltpu.make_async_remote_copy(
            src_ref=s3.at[to], dst_ref=r3.at[k - 1],
            send_sem=s3_send.at[k - 1], recv_sem=s3_recv.at[k - 1],
            device_id=(2 * to + core, b), device_id_type=MESH,
        )
        cp.start()
        third.append(cp)
    total = own3[z]
    for k in range(1, nz):
        third[k - 1].wait_recv()
        total = total + r3[k - 1].astype(F32)[0:cw]
    grad_ref[...] = total * cfg["factor"]

    for cp in gathers + forwards + list(first.values()) + list(second.values()) + third:
        cp.wait_send()


def per_device(tiles, cotangent, halo_flags, send_plan, spatial_weight, temporal_weight):
    nd, nb = lax.axis_size("dp"), lax.axis_size("bal")
    owned, cells, C = tiles.shape
    opix = cotangent.shape[1]
    rs, rt = spatial_weight.shape[0], temporal_weight.shape[0]
    S = up(owned, 8)
    nt = max(-(-(rs * (n + 1)) // 128) - rs * n // 128 for n in range(nb))
    sp_lanes = nt * 128
    nl = sp_lanes + 128
    cw = C // nd
    cwp = up(cw, 16)
    nz = nd // 2
    half = C // 2
    n_parts = 4
    parts = [owned // n_parts + (n < owned % n_parts) for n in range(n_parts)]
    cfg = dict(
        nd=nd, nb=nb, owned=owned, C=C, S=S, rs=rs, rt=rt, nt=nt, nl=nl, cw=cw, cwp=cwp,
        parts=parts, factor=1.0 / math.sqrt(nd * nb * WORK_TILES),
    )
    M = FR * TR * TC * S
    K = TO * TR * TC * S
    vm = pltpu.VMEM
    dma = pltpu.SemaphoreType.DMA
    any_spec = pl.BlockSpec(memory_space=pl.ANY)
    vspec = pl.BlockSpec(memory_space=pltpu.VMEM)
    scratch = [
        vm((owned, cells, C), BF16),
        vm((2, S * (cells + 1), 128), F32),
        vm((2, S * (opix + 1), 128), F32),
        vm((M, 9 * C), BF16),
        vm((K, C), BF16),
        vm((9 * C, C), BF16),
        vm((2 * C, C), BF16),
        vm((M, C), BF16),
        vm((8, 128), F32),
        vm((C, M), BF16),
        vm((C, K), BF16),
        vm((S, 128), F32),
        vm((3, S, 128), F32),
        vm((nb, half, nl), F32),
        vm((nb, half, nl), BF16),
        vm((nb, half, nl), BF16),
        vm((nb - 1, half, nl), BF16),
        vm((nb - 1, half, nl), BF16),
        vm((nz, cw, nl), F32),
        vm((nz, cwp, nl), BF16),
        vm((nz - 1, cwp, nl), BF16),
        dma((n_parts,)),
        dma((2,)),
        dma((2, nb - 1)), dma((2, nb - 1)), dma((2, nb - 1)), dma((2, nb - 1)),
        dma((nb,)), dma((nb,)),
        dma((nb - 1,)), dma((nb - 1,)),
        dma((nz - 1,)), dma((nz - 1,)),
    ]
    features, grads = pl.pallas_call(
        functools.partial(kernel, cfg),
        out_shape=(
            jax.ShapeDtypeStruct((owned, opix, C), BF16),
            jax.ShapeDtypeStruct((cw, nl), F32),
        ),
        in_specs=[
            any_spec, vspec, vspec, pl.BlockSpec(memory_space=pltpu.SMEM), any_spec, any_spec,
        ],
        out_specs=(vspec, vspec),
        scratch_shapes=scratch,
        compiler_params=pltpu.CompilerParams(
            collective_id=0, has_side_effects=True, vmem_limit_bytes=50 * 1024 * 1024
        ),
    )(tiles, cotangent, halo_flags, send_plan, spatial_weight, temporal_weight)
    b = lax.axis_index("bal")
    sp = lax.dynamic_slice(grads, (0, lax.rem(b * rs, 128)), (cw, rs)).T
    tp = lax.dynamic_slice(grads, (0, sp_lanes + lax.rem(b * rt, 128)), (cw, rt)).T
    return (features, sp, tp)


def solution(mesh):
    in_specs = (
        P(("dp", "bal"), None, None),
        P(("dp", "bal"), None, None),
        P(("dp", "bal"), None),
        P(("dp", "bal"), None, None),
        P("bal", None),
        P("bal", None),
    )
    out_specs = (P(("dp", "bal"), None, None), P("bal", "dp"), P("bal", "dp"))
    return jax.shard_map(
        per_device, mesh=mesh, in_specs=in_specs, out_specs=out_specs, check_vma=False
    )
```

time: 184 us -> 45.2 us (0.25)
  waiting for transfers between devices: 118 us -> 0 us
  Pallas kernels: 0 us -> 37.9 us
  local copies, waits for them, and re-layouts: 21 us -> 6.32 us
  between operations: 13.9 us -> 0.65 us
  blocking collectives: 12.4 us -> 0 us
  matrix products: 11.9 us -> 0 us
  other arithmetic: 5.83 us -> 0 us
    reduce_scatter x3 -> x0, waiting for transfers between devices: 85 us -> none  [the longest x1 36.8 us: per_device(): lax.psum_scatter(grad_space, 'dp', scatter_dimension=1, tiled=True)]
    pallas_call x0 -> x1, Pallas kernels: none -> 37.9 us  [per_device(): pl.pallas_call(functools.partial(kernel, cfg), out_shape=(jax.ShapeDtypeS...]
    unnamed x6 -> x0, waiting for transfers between devices: 30.8 us -> none
    all_gather x1 -> x0, blocking collectives: 12.4 us -> none  [per_device(): lax.all_gather(temporal_weight, 'bal', axis=0, tiled=True)]
    dot_general x5 -> x0, matrix products: 11.9 us -> none  [the longest x1 5.64 us: tile_pass(): lax.dot_general(patches, grad_pre, (((0,), (0,)), ((), ())), preferred_el...]
    reshape x1 -> x0, local copies, waits for them, and re-layouts: 8.9 us -> none  [tile_pass(): patches = jnp.concatenate(tap_list, axis=-1).reshape(-1, 9 * channel_index)]
    concatenate x2 -> x0, local copies, waits for them, and re-layouts: 4.33 us -> none  [tile_pass(): patches = jnp.concatenate(tap_list, axis=-1).reshape(-1, 9 * channel_index)]
    unnamed x17 -> x10, local copies, waits for them, and re-layouts: 7.41 us -> 4.98 us
  transfers between devices with their start and end apart: 5 -> 0, of which waited for: 5 -> 0; matrix products, arithmetic and copies ran while one was open for 16% -> 0% of each run, Pallas kernels for 0% -> 0%
where the time goes in v1:
time: 45.2 us; the launch traced here: 44.9 us
  Pallas kernels  37.9 us (84%)
  local copies, waits for them, and re-layouts  6.32 us (14%)
  between operations  0.65 us (1%)
    pallas_call x1, Pallas kernels, per_device(): pl.pallas_call(functools.partial(kernel, cfg), out_shape=(jax.ShapeDtypeS...  37.9 us
    unnamed x10, local copies, waits for them, and re-layouts  4.98 us

profile of v1, /device:TPU:0, one launch (start us, length us, event | category | flops | bytes accessed | tf_op | source)
XLA Modules:
  0.0 44.9 jit_solution(7678370983530084234)
XLA Ops:
  0.6 0.8 %copy.9.flags_ref = s32[23,3]{1,0:T(8,128)S(1)} copy(s32[23,3]{0,1:T(4,128)} %param.8) | data formatting | bytes 552 | tf_op args[2]
  1.4 0.0 copy-start
  1.4 1.0 %copy-done = bf16[23,32,256]{2,1,0:T(8,128)(2,1)S(1)} copy-done((bf16[23,32,256]{2,1,0:T(8,128)(2,1)S(1)}, bf16[23,32,256]{2,1,0:T(8,128)(2,1)}, u32[]{:S(2)}) %copy-start) | copy-done | bytes 376856
  2.4 0.0 copy-start.1
  2.4 1.0 %copy-done.1 = bf16[576,256]{1,0:T(8,128)(2,1)S(1)} copy-done((bf16[576,256]{1,0:T(8,128)(2,1)S(1)}, bf16[576,256]{1,0:T(8,128)(2,1)}, u32[]{:S(2)}) %copy-start.1) | copy-done | bytes 294936
  3.4 0.0 copy-start.2
  3.4 0.8 %copy-done.2 = bf16[128,256]{1,0:T(8,128)(2,1)S(1)} copy-done((bf16[128,256]{1,0:T(8,128)(2,1)S(1)}, bf16[128,256]{1,0:T(8,128)(2,1)}, u32[]{:S(2)}) %copy-start.2) | copy-done | bytes 65560
  4.2 0.0 copy-start.3
  4.2 0.7 %copy-done.3 = s32[1,4,6]{2,1,0:T(4,128)S(1)} copy-done((s32[1,4,6]{2,1,0:T(4,128)S(1)}, s32[1,4,6]{2,1,0:T(4,128)}, u32[]{:S(2)}) %copy-start.3) | copy-done | bytes 120
  4.9 37.9 %shard_map.85 = (bf16[23,32,256]{2,1,0:T(8,128)(2,1)S(1)}, f32[32,768]{1,0:T(8,128)S(1)}) custom-call(bf16[23,270,256]{2,1,0:T(8,128)(2,1)} %tiles_ref.1, bf16[23,32,256]{2,1,0:T(8,128)(2,1)S(1)} %copy-done, s32[23,3]{1,0:T(8,128)S(1)} %copy.9.flags_ref, s32[1,4,6]{2,1,0:T(4,128)S(1)} %copy-done.3, bf16[576,256]{1,0:T(8,128)(2,1)S(1)} %copy-done.1, ...), custom_call_target="tpu_custom_call" | custom-call | tf_op jit(solution)/shard_map/pallas_call | solution.py:395
  42.8 0.7 %dynamic-slice_bitcast_fusion = f32[576,32]{0,1:T(8,128)} fusion(f32[32,768]{1,0:T(8,128)S(1)} %get-tuple-element.6, s32[]{:T(128)S(6)} %select_n.6), kind=kLoop, calls=%fused_computation | loop fusion | bytes 147460 | tf_op jit(solution)/shard_map/transpose | solution.py:411
  43.6 0.6 %dynamic-slice_bitcast_fusion.1 = f32[128,32]{0,1:T(8,128)} fusion(f32[32,768]{1,0:T(8,128)S(1)} %get-tuple-element.6, s32[]{:T(128)S(6)} %select_n.7), kind=kLoop, calls=%fused_computation.1 | loop fusion | bytes 32772 | tf_op jit(solution)/shard_map/transpose | solution.py:412
  44.2 0.7 %copy.11 = bf16[23,32,256]{2,1,0:T(8,128)(2,1)} copy(bf16[23,32,256]{2,1,0:T(8,128)(2,1)S(1)} %get-tuple-element.10) | data formatting | bytes 753664
Async XLA Ops:
  1.4 1.0 %copy-start = (bf16[23,32,256]{2,1,0:T(8,128)(2,1)S(1)}, bf16[23,32,256]{2,1,0:T(8,128)(2,1)}, u32[]{:S(2)}) copy-start(bf16[23,32,256]{2,1,0:T(8,128)(2,1)} %cot_ref.1) | copy-start | bytes 1130500
  2.4 1.0 %copy-start.1 = (bf16[576,256]{1,0:T(8,128)(2,1)S(1)}, bf16[576,256]{1,0:T(8,128)(2,1)}, u32[]{:S(2)}) copy-start(bf16[576,256]{1,0:T(8,128)(2,1)} %wsp_ref.1) | copy-start | bytes 884740
  3.4 0.8 %copy-start.2 = (bf16[128,256]{1,0:T(8,128)(2,1)S(1)}, bf16[128,256]{1,0:T(8,128)(2,1)}, u32[]{:S(2)}) copy-start(bf16[128,256]{1,0:T(8,128)(2,1)} %wtp_ref.1) | copy-start | bytes 196612
  4.2 0.7 %copy-start.3 = (s32[1,4,6]{2,1,0:T(4,128)S(1)}, s32[1,4,6]{2,1,0:T(4,128)}, u32[]{:S(2)}) copy-start(s32[1,4,6]{2,1,0:T(4,128)} %plan_ref.1) | copy-start | bytes 292

commit v2 on v1

v2 whole, which is shorter than its diff:
```python
import functools
import math

import jax
import jax.numpy as jnp
from jax import lax
from jax.experimental import pallas as pl
from jax.experimental.pallas import tpu as pltpu
from jax.sharding import PartitionSpec as P

FR, H, W = 6, 5, 9
TR, TC, TO = 2, 4, 4
WORK_TILES = 12
F32, BF16 = jnp.float32, jnp.bfloat16
MESH = pl.DeviceIdType.MESH


def up(value, step):
    return (value + step - 1) // step * step


def kernel(
    cfg,
    tiles_ref, cot_ref, flags_ref, plan_ref, wsp_ref, wtp_ref,
    feat_ref, grad_ref,
    cbuf, fbuf, pbuf, ftmp, tbuf, xf, cf, patches, cotp, wsp, wtp, act, dact, grad_t, cot_t, live, masks,
    own, s1, r1, s2, r2, own3, s3, r3,
    tile_sem, loc_sem, ag_send, ag_recv, zr_send, zr_recv, fw_send, fw_recv,
    s1_send, s1_recv, s2_send, s2_recv, s3_send, s3_recv,
):
    nd, nb, owned, C = cfg["nd"], cfg["nb"], cfg["owned"], cfg["C"]
    S, rs, rt, nt, nl = cfg["S"], cfg["rs"], cfg["rt"], cfg["nt"], cfg["nl"]
    cw, cwp, parts = cfg["cw"], cfg["cwp"], cfg["parts"]
    nz = nd // 2
    cells, opix = FR * H * W, TO * TR * TC
    ts, cs = cells + 1, opix + 1
    FS = TR * TC * S
    half = C // 2

    d = lax.axis_index("dp")
    b = lax.axis_index("bal")
    core = lax.rem(d, 2)
    z = d // 2
    mate = d + 1 - 2 * core

    def bal_peer(k):
        return lax.rem(b + k, nb)

    def z_peer(k):
        return lax.rem(z + k, nz)

    def local_copy(src, dst, sem):
        cp = pltpu.make_async_copy(src, dst, sem)
        cp.start()
        return cp

    barrier = pltpu.get_barrier_semaphore()
    pl.semaphore_signal(barrier, inc=1, device_id=(mate, b), device_id_type=MESH)
    for k in range(1, nb):
        pl.semaphore_signal(barrier, inc=1, device_id=(d, bal_peer(k)), device_id_type=MESH)
    for k in range(1, nz):
        pl.semaphore_signal(
            barrier, inc=1, device_id=(2 * z_peer(k) + core, b), device_id_type=MESH
        )

    small_copies = [
        local_copy(flags_ref, fbuf, loc_sem.at[2]),
        local_copy(plan_ref, pbuf, loc_sem.at[3]),
        local_copy(cot_ref, cbuf, loc_sem.at[4]),
    ]
    tile_copies = []
    lo = 0
    for n, count in enumerate(parts):
        part = pl.ds(lo, count)
        cp = local_copy(tiles_ref.at[part], tbuf.at[part], tile_sem.at[n])
        tile_copies.append((cp, lo, count))
        lo += count
    my_sp = pl.ds(pl.multiple_of(b * rs, 16), rs)
    my_tp = pl.ds(pl.multiple_of(b * rt, 16), rt)
    local = [
        local_copy(wsp_ref, wsp.at[my_sp], loc_sem.at[0]),
        local_copy(wtp_ref, wtp.at[my_tp], loc_sem.at[1]),
    ]

    if S > owned:
        for h in range(2):
            cf[h, owned * cs : S * cs, :] = jnp.zeros(((S - owned) * cs, 128), F32)
            xf[h, owned * ts : S * ts, :] = jnp.zeros(((S - owned) * ts, 128), F32)

    pl.semaphore_wait(barrier, nb + nz - 1)

    lanes = pl.ds(pl.multiple_of(core * half, 128), half)
    zpar = lax.rem(z, 2)
    zmate = 2 * (z + 1 - 2 * zpar) + core
    weights = []
    for src, dst, size in ((wsp_ref, wsp, rs), (wtp_ref, wtp, rt)):
        units = size // 16
        fetch = units if nz % 2 else max((units + 1) // 2, round(0.6 * units))
        weights.append((src, dst, size, fetch * 16, (units - fetch) * 16))

    def rows_at(start, count):
        return pl.ds(pl.multiple_of(start, 16), count)

    gathers, relays, forwards = {}, {}, {}
    for k in range(1, nb):
        for n, (src, dst, size, fetch, rest) in enumerate(weights):
            cp = pltpu.make_async_remote_copy(
                src_ref=src.at[rows_at(zpar * rest, fetch), lanes],
                dst_ref=dst.at[rows_at(b * size + zpar * rest, fetch), lanes],
                send_sem=ag_send.at[n, k - 1],
                recv_sem=ag_recv.at[n, k - 1],
                device_id=(d, bal_peer(k)),
                device_id_type=MESH,
            )
            cp.start()
            gathers[n, k] = cp

    def push(ref, rows, to, send, recv):
        cp = pltpu.make_async_remote_copy(
            src_ref=ref.at[rows, lanes], dst_ref=ref.at[rows, lanes],
            send_sem=send, recv_sem=recv, device_id=(to, b), device_id_type=MESH,
        )
        cp.start()
        return cp

    def relay(k):
        origin = lax.rem(b + nb - k, nb)
        for n, (src, dst, size, fetch, rest) in enumerate(weights):
            gathers[n, k].wait_recv()
            if rest:
                relays[n, k] = push(
                    dst, rows_at(origin * size + zpar * fetch, rest), zmate,
                    zr_send.at[n, k - 1], zr_recv.at[n, k - 1],
                )
            forwards[0, n, k] = push(
                dst, rows_at(origin * size + zpar * rest, fetch), mate,
                fw_send.at[0, n, k - 1], fw_recv.at[0, n, k - 1],
            )

    def relay_rest(k):
        origin = lax.rem(b + nb - k, nb)
        for n, (src, dst, size, fetch, rest) in enumerate(weights):
            if rest:
                relays[n, k].wait_recv()
                forwards[1, n, k] = push(
                    dst, rows_at(origin * size + (1 - zpar) * fetch, rest), mate,
                    fw_send.at[1, n, k - 1], fw_recv.at[1, n, k - 1],
                )

    for cp in small_copies:
        cp.wait()
    slot = lax.broadcasted_iota(jnp.int32, (S, 128), 0)
    lane = lax.broadcasted_iota(jnp.int32, (S, 128), 1)
    ftmp[...] = jnp.zeros_like(ftmp)
    ftmp[0:3, 0:owned] = (fbuf[...] > 0).astype(F32)
    for n in range(3):
        row = jnp.broadcast_to(ftmp[n : n + 1, :], (S, 128))
        column = jnp.sum(jnp.where(slot == lane, row, 0.0), axis=1, keepdims=True)
        masks[n] = jnp.broadcast_to(column, (S, 128))
    found = jnp.zeros((S, 128), F32)
    for w in range(pbuf.shape[1]):
        for q in range(pbuf.shape[2]):
            found = jnp.maximum(found, jnp.where(slot == pbuf[0, w, q], 1.0, 0.0))
    live[...] = found

    def cot_in(s, carry):
        v = cbuf[s].astype(F32)
        for h in range(2):
            cf[h, pl.ds(s * cs, opix), :] = v[:, h * 128 : (h + 1) * 128]
        return carry

    lax.fori_loop(0, owned, cot_in, 0)
    lv = live[...]

    def cot_rows(p, carry):
        for h in range(2):
            pair = [
                cf[h, pl.ds(2 * p + n, S, stride=cs), :] * lv for n in range(2)
            ]
            cotp[pl.ds(pl.multiple_of(p * 2 * S, 16), 2 * S), h * 128 : (h + 1) * 128] = (
                jnp.concatenate(pair, axis=0).astype(BF16)
            )
        return carry

    lax.fori_loop(0, opix // 2, cot_rows, 0)

    def split_rows(v):
        cores = [
            jnp.concatenate(
                [v[(2 * n + q) * cw : (2 * n + q + 1) * cw] for n in range(nz)], axis=0
            )
            for q in range(2)
        ]
        return cores

    def store_split(ref, v, lo, width):
        cores = split_rows(v)
        for q in range(2):
            at = core if q == 1 else 0
            at = (1 - core) if q == 1 else core
            ref[pl.ds(pl.multiple_of(at * half, 128), half), lo : lo + width] = cores[
                q
            ].astype(BF16)

    for n in range(2):
        rows = n * 2 * FS
        store_split(cot_t, cotp[rows : rows + 2 * FS, :].astype(F32).T, rows, 2 * FS)

    def tile_in(s, carry):
        v = tbuf[s].astype(F32)
        for h in range(2):
            xf[h, pl.ds(s * ts, cells), :] = v[:, h * 128 : (h + 1) * 128]
        return carry

    for cp, lo, count in tile_copies:
        cp.wait()
        lax.fori_loop(lo, lo + count, tile_in, 0)

    top, left, past = masks[0], masks[1], masks[2]

    def patch_rows(f, carry):
        hist = jnp.where(f >= 2, jnp.ones_like(past), past)
        hist_top, hist_left = hist * top, hist * left
        hist_both = hist_top * left
        for i in range(TR):
            for jp in range(TC // 2):
                row = pl.ds(pl.multiple_of(f * FS + (i * TC + 2 * jp) * S, 16), 2 * S)
                for ky in range(3):
                    for kx in range(3):
                        on_top = 2 * i + ky == 0
                        on_left = jp == 0 and kx == 0
                        first = (
                            hist_both if on_top and on_left
                            else hist_top if on_top
                            else hist_left if on_left
                            else hist
                        )
                        second = hist_top if on_top else hist
                        cell = f * (H * W) + (2 * i + ky) * W + 4 * jp + kx
                        tap = 3 * ky + kx
                        for h in range(2):
                            v0 = xf[h, pl.ds(cell, S, stride=ts), :] * first
                            v1 = xf[h, pl.ds(cell + 2, S, stride=ts), :] * second
                            patches[row, tap * C + h * 128 : tap * C + (h + 1) * 128] = (
                                jnp.concatenate([v0, v1], axis=0).astype(BF16)
                            )
        return carry

    steps = max(nb - 1, 1)
    cuts = [FR * n // steps for n in range(steps + 1)]
    for n in range(steps):
        if cuts[n + 1] > cuts[n]:
            lax.fori_loop(cuts[n], cuts[n + 1], patch_rows, 0)
        if n + 1 < nb:
            relay(n + 1)
    for k in range(1, nb):
        relay_rest(k)
    for cp in local:
        cp.wait()
    for cp in forwards.values():
        cp.wait_recv()

    def chunk(n):
        rows = n * 2 * FS
        pre = jnp.dot(patches[rows : rows + 2 * FS, :], wsp[...], preferred_element_type=F32)
        sig = 1.0 / (1.0 + jnp.exp(-pre))
        act[rows : rows + 2 * FS, :] = (pre * sig).astype(BF16)
        ga = None
        nt_dims = (((1,), (1,)), ((), ()))
        if n > 0:
            lo = (n - 1) * 2 * FS
            ga = lax.dot_general(
                cotp[lo : lo + 2 * FS, :], wtp[0:C, :], nt_dims, preferred_element_type=F32
            )
        if n < 2:
            g = lax.dot_general(
                cotp[rows : rows + 2 * FS, :], wtp[C : 2 * C, :], nt_dims,
                preferred_element_type=F32,
            )
            ga = g if ga is None else ga + g
        gp = ga * (sig * (1.0 + pre * (1.0 - sig)))
        store_split(grad_t, gp.T, rows, 2 * FS)

    for n in range(3):
        chunk(n)

    sp_lanes = nt * 128
    cut = (nt + 2) // 2
    spans = [(0, cut), (cut, nt)]
    bounds = [pl.ds(0, cut * 128), pl.ds(cut * 128, nl - cut * 128)]

    def section(h, k):
        to = bal_peer(k)
        lo, hi = spans[h]
        if hi > lo:
            sp_at = pl.multiple_of((to * rs) // 128 * 128 + lo * 128, 128)
            g = jnp.dot(
                grad_t[...], patches[:, pl.ds(sp_at, (hi - lo) * 128)],
                preferred_element_type=F32,
            )
            own[k - 1, :, lo * 128 : hi * 128] = g[0:half]
            s1[k - 1, :, lo * 128 : hi * 128] = g[half:].astype(BF16)
        if h == 1:
            tp_at = (to * rt) // 128 * 128
            tap = tp_at // C
            at = pl.multiple_of(tp_at - tap * C, 128)
            rows = pl.ds(pl.multiple_of((1 - tap) * 2 * FS, 16), TO * FS)
            g = jnp.dot(cot_t[...], act[rows, pl.ds(at, 128)], preferred_element_type=F32)
            own[k - 1, :, sp_lanes:] = g[0:half]
            s1[k - 1, :, sp_lanes:] = g[half:].astype(BF16)
        cp = pltpu.make_async_remote_copy(
            src_ref=s1.at[k - 1, :, bounds[h]], dst_ref=r1.at[k - 1, :, bounds[h]],
            send_sem=s1_send.at[h, k - 1], recv_sem=s1_recv.at[h, k - 1],
            device_id=(mate, b), device_id_type=MESH,
        )
        cp.start()
        first[h, k] = cp

    first, second, third = {}, {}, {}

    def pass_on(h, k):
        first[h, k].wait_recv()
        at = bounds[h]
        total = own[k - 1, :, at] + r1[k - 1, :, at].astype(F32)
        if k == nb:
            own[k - 1, :, at] = total
            return
        s2[k - 1, :, at] = total.astype(BF16)
        cp = pltpu.make_async_remote_copy(
            src_ref=s2.at[k - 1, :, at], dst_ref=r2.at[k - 1, :, at],
            send_sem=s2_send.at[h, k - 1], recv_sem=s2_recv.at[h, k - 1],
            device_id=(d, bal_peer(k)), device_id_type=MESH,
        )
        cp.start()
        second[h, k] = cp

    order = [(h, k) for h in range(2) for k in range(1, nb + 1)]
    for n, unit in enumerate(order):
        section(*unit)
        if n > 0:
            pass_on(*order[n - 1])
    pass_on(*order[-1])

    def features(t0):
        rows = t0 * FS
        feat = jnp.dot(
            act[rows + 2 * FS : rows + 4 * FS, :], wtp[0:C, :], preferred_element_type=F32
        ) + jnp.dot(act[rows : rows + 2 * FS, :], wtp[C : 2 * C, :], preferred_element_type=F32)
        for p in range(2 * TR * TC):
            for h in range(2):
                v = feat[p * S : (p + 1) * S, h * 128 : (h + 1) * 128]
                cf[h, pl.ds(t0 * TR * TC + p, S, stride=cs), :] = v * lv

    def group_sum(h):
        at = bounds[h]
        total = own[nb - 1, :, at]
        for k in range(1, nb):
            second[h, k].wait_recv()
            total = total + r2[k - 1, :, at].astype(F32)
        for n in range(nz):
            part = total[n * cw : (n + 1) * cw]
            own3[n, :, at] = part
            if cwp > cw:
                part = jnp.concatenate(
                    [part, jnp.zeros((cwp - cw, part.shape[1]), F32)], axis=0
                )
            s3[n, :, at] = part.astype(BF16)
        for k in range(1, nz):
            to = z_peer(k)
            cp = pltpu.make_async_remote_copy(
                src_ref=s3.at[to, :, at], dst_ref=r3.at[k - 1, :, at],
                send_sem=s3_send.at[h, k - 1], recv_sem=s3_recv.at[h, k - 1],
                device_id=(2 * to + core, b), device_id_type=MESH,
            )
            cp.start()
            third[h, k] = cp

    features(0)
    features(2)
    group_sum(0)

    def feat_out(s, carry):
        cbuf[s] = jnp.concatenate(
            [cf[h, pl.ds(s * cs, opix), :] for h in range(2)], axis=1
        ).astype(BF16)
        return carry

    lax.fori_loop(0, owned, feat_out, 0)
    feat_copy = local_copy(cbuf, feat_ref, loc_sem.at[5])
    group_sum(1)
    for h in range(2):
        at = bounds[h]
        total = own3[z, :, at]
        for k in range(1, nz):
            third[h, k].wait_recv()
            total = total + r3[k - 1, :, at].astype(F32)[0:cw]
        grad_ref[:, at] = total * cfg["factor"]

    feat_copy.wait()
    for group in (gathers, relays, forwards, first, second, third):
        for cp in group.values():
            cp.wait_send()


def per_device(tiles, cotangent, halo_flags, send_plan, spatial_weight, temporal_weight):
    nd, nb = lax.axis_size("dp"), lax.axis_size("bal")
    owned, cells, C = tiles.shape
    opix = cotangent.shape[1]
    rs, rt = spatial_weight.shape[0], temporal_weight.shape[0]
    S = up(owned, 8)
    nt = max(-(-(rs * (n + 1)) // 128) - rs * n // 128 for n in range(nb))
    sp_lanes = nt * 128
    nl = sp_lanes + 128
    cw = C // nd
    cwp = up(cw, 16)
    nz = nd // 2
    half = C // 2
    n_parts = 4
    parts = [owned // n_parts + (n < owned % n_parts) for n in range(n_parts)]
    cfg = dict(
        nd=nd, nb=nb, owned=owned, C=C, S=S, rs=rs, rt=rt, nt=nt, nl=nl, cw=cw, cwp=cwp,
        parts=parts, factor=1.0 / math.sqrt(nd * nb * WORK_TILES),
    )
    M = FR * TR * TC * S
    K = TO * TR * TC * S
    vm = pltpu.VMEM
    dma = pltpu.SemaphoreType.DMA
    hbm = pl.BlockSpec(memory_space=pltpu.HBM)
    vspec = pl.BlockSpec(memory_space=pltpu.VMEM)
    scratch = [
        vm((owned, opix, C), BF16),
        vm((3, owned), jnp.int32),
        pltpu.SMEM(send_plan.shape, jnp.int32),
        vm((8, 128), F32),
        vm((owned, cells, C), BF16),
        vm((2, S * (cells + 1), 128), F32),
        vm((2, S * (opix + 1), 128), F32),
        vm((M, 9 * C), BF16),
        vm((K, C), BF16),
        vm((9 * C, C), BF16),
        vm((2 * C, C), BF16),
        vm((M, C), BF16),
        vm((8, 128), F32),
        vm((C, M), BF16),
        vm((C, K), BF16),
        vm((S, 128), F32),
        vm((3, S, 128), F32),
        vm((nb, half, nl), F32),
        vm((nb, half, nl), BF16),
        vm((nb, half, nl), BF16),
        vm((nb - 1, half, nl), BF16),
        vm((nb - 1, half, nl), BF16),
        vm((nz, cw, nl), F32),
        vm((nz, cwp, nl), BF16),
        vm((nz - 1, cwp, nl), BF16),
        dma((n_parts,)),
        dma((6,)),
        dma((2, nb - 1)), dma((2, nb - 1)), dma((2, nb - 1)), dma((2, nb - 1)),
        dma((2, 2, nb - 1)), dma((2, 2, nb - 1)),
        dma((2, nb)), dma((2, nb)),
        dma((2, nb - 1)), dma((2, nb - 1)),
        dma((2, nz - 1)), dma((2, nz - 1)),
    ]
    features, grads = pl.pallas_call(
        functools.partial(kernel, cfg),
        out_shape=(
            jax.ShapeDtypeStruct((owned, opix, C), BF16),
            jax.ShapeDtypeStruct((cw, nl), F32),
        ),
        in_specs=[hbm] * 6,
        out_specs=(hbm, vspec),
        scratch_shapes=scratch,
        compiler_params=pltpu.CompilerParams(
            collective_id=0, has_side_effects=True, vmem_limit_bytes=64 * 1024 * 1024 - 65536
        ),
    )(tiles, cotangent, halo_flags.T, send_plan, spatial_weight, temporal_weight)
    b = lax.axis_index("bal")
    sp = lax.dynamic_slice(grads, (0, lax.rem(b * rs, 128)), (cw, rs)).T
    tp = lax.dynamic_slice(grads, (0, sp_lanes + lax.rem(b * rt, 128)), (cw, rt)).T
    return (features, sp, tp)


def solution(mesh):
    in_specs = (
        P(("dp", "bal"), None, None),
        P(("dp", "bal"), None, None),
        P(("dp", "bal"), None),
        P(("dp", "bal"), None, None),
        P("bal", None),
        P("bal", None),
    )
    out_specs = (P(("dp", "bal"), None, None), P("bal", "dp"), P("bal", "dp"))
    return jax.shard_map(
        per_device, mesh=mesh, in_specs=in_specs, out_specs=out_specs, check_vma=False
    )
```

time: 45.2 us -> 42 us (0.929)
  local copies, waits for them, and re-layouts: 6.32 us -> 4.7 us
  Pallas kernels: 37.9 us -> 36.4 us
    unnamed x10 -> x1, local copies, waits for them, and re-layouts: 4.98 us -> 1.75 us
    pallas_call x1, Pallas kernels: 37.9 us -> 36.4 us  [per_device(): pl.pallas_call(functools.partial(kernel, cfg), out_shape=(jax.ShapeDtypeS...]
    transpose x1, local copies, waits for them, and re-layouts: 0.73 us -> 1.63 us  [per_device(): sp = lax.dynamic_slice(grads, (0, lax.rem(b * rs, 128)), (cw, rs)).T]
    transpose x1, local copies, waits for them, and re-layouts: 0.61 us -> 1.32 us  [per_device(): lax.dynamic_slice(grads, (0, sp_lanes + lax.rem(b * rt, 128)), (cw, rt))]
where the time goes in v2:
time: 42 us; the launch traced here: 41.8 us
  Pallas kernels  36.4 us (87%)
  local copies, waits for them, and re-layouts  4.7 us (11%)
  between operations  0.65 us (2%)
    pallas_call x1, Pallas kernels, per_device(): pl.pallas_call(functools.partial(kernel, cfg), out_shape=(jax.ShapeDtypeS...  36.4 us
    unnamed x1, local copies, waits for them, and re-layouts  1.75 us
    transpose x1, local copies, waits for them, and re-layouts, per_device(): sp = lax.dynamic_slice(grads, (0, lax.rem(b * rs, 128)), (cw, rs)).T  1.63 us
    transpose x1, local copies, waits for them, and re-layouts, per_device(): lax.dynamic_slice(grads, (0, sp_lanes + lax.rem(b * rt, 128)), (cw, rt))  1.32 us

profile of v2, /device:TPU:0, one launch (start us, length us, event | category | flops | bytes accessed | tf_op | source)
XLA Modules:
  0.0 41.8 jit_solution(2051790311021985953)
XLA Ops:
  0.6 36.4 %shard_map.85 = (bf16[23,32,256]{2,1,0:T(8,128)(2,1)}, f32[32,768]{1,0:T(8,128)}) custom-call(bf16[23,270,256]{2,1,0:T(8,128)(2,1)} %tiles_ref.1, bf16[23,32,256]{2,1,0:T(8,128)(2,1)} %cot_ref.1, s32[3,23]{1,0:T(4,128)} %bitcast.5, s32[1,4,6]{2,1,0:T(4,128)} %plan_ref.1, bf16[576,256]{1,0:T(8,128)(2,1)} %wsp_ref.1, bf16[128,256]{1,0:T(8,128)(2,1)} %wtp_ref.1), custom_call_target="tpu_custom_call" | custom-call | tf_op jit(solution)/shard_map/pallas_call | solution.py:464
  37.1 1.6 %dynamic-slice_bitcast_fusion = f32[576,32]{0,1:T(8,128)} fusion(f32[32,768]{1,0:T(8,128)} %get-tuple-element.6, s32[]{:T(128)S(6)} %select_n.6), kind=kLoop, calls=%fused_computation | loop fusion | bytes 147460 | tf_op jit(solution)/shard_map/transpose | solution.py:478
  38.7 1.3 %dynamic-slice_bitcast_fusion.1 = f32[128,32]{0,1:T(8,128)} fusion(f32[32,768]{1,0:T(8,128)} %get-tuple-element.6, s32[]{:T(128)S(6)} %select_n.7), kind=kLoop, calls=%fused_computation.1 | loop fusion | bytes 32772 | tf_op jit(solution)/shard_map/transpose | solution.py:479
  40.0 1.8 %copy.10 = bf16[23,32,256]{2,1,0:T(8,128)(2,1)} copy(bf16[23,32,256]{2,1,0:T(8,128)(2,1)} %get-tuple-element.10) | data formatting | bytes 753664

commit v3 on v2

--- a/solution.py
+++ b/solution.py
@@ -222,38 +222,38 @@
         hist = jnp.where(f >= 2, jnp.ones_like(past), past)
         hist_top, hist_left = hist * top, hist * left
         hist_both = hist_top * left
-        for i in range(TR):
-            for jp in range(TC // 2):
-                row = pl.ds(pl.multiple_of(f * FS + (i * TC + 2 * jp) * S, 16), 2 * S)
-                for ky in range(3):
-                    for kx in range(3):
-                        on_top = 2 * i + ky == 0
-                        on_left = jp == 0 and kx == 0
-                        first = (
-                            hist_both if on_top and on_left
-                            else hist_top if on_top
-                            else hist_left if on_left
-                            else hist
-                        )
-                        second = hist_top if on_top else hist
-                        cell = f * (H * W) + (2 * i + ky) * W + 4 * jp + kx
-                        tap = 3 * ky + kx
-                        for h in range(2):
-                            v0 = xf[h, pl.ds(cell, S, stride=ts), :] * first
-                            v1 = xf[h, pl.ds(cell + 2, S, stride=ts), :] * second
-                            patches[row, tap * C + h * 128 : tap * C + (h + 1) * 128] = (
-                                jnp.concatenate([v0, v1], axis=0).astype(BF16)
+        for r in range(H):
+            uses = [(r - 2 * i, i) for i in range(TR) if 0 <= r - 2 * i < 3]
+            mask = hist_top if r == 0 else hist
+            mask_left = hist_both if r == 0 else hist_left
+            for h in range(2):
+                cols = [
+                    xf[h, pl.ds(f * (H * W) + r * W + c, S, stride=ts), :]
+                    * (mask_left if c == 0 else mask)
+                    for c in range(W)
+                ]
+                for kx in range(3):
+                    for jp in range(TC // 2):
+                        c = 4 * jp + kx
+                        v = jnp.concatenate([cols[c], cols[c + 2]], axis=0).astype(BF16)
+                        for ky, i in uses:
+                            row = pl.ds(
+                                pl.multiple_of(f * FS + (i * TC + 2 * jp) * S, 16), 2 * S
                             )
+                            at = (3 * ky + kx) * C + h * 128
+                            patches[row, at : at + 128] = v
         return carry
 
     steps = max(nb - 1, 1)
     cuts = [FR * n // steps for n in range(steps + 1)]
     for n in range(steps):
+        if n + 1 < nb:
+            relay(n + 1)
+        if n > 1:
+            relay_rest(n - 1)
         if cuts[n + 1] > cuts[n]:
             lax.fori_loop(cuts[n], cuts[n + 1], patch_rows, 0)
-        if n + 1 < nb:
-            relay(n + 1)
-    for k in range(1, nb):
+    for k in range(max(steps - 1, 1), nb):
         relay_rest(k)
     for cp in local:
         cp.wait()
@@ -335,11 +335,13 @@
         second[h, k] = cp
 
     order = [(h, k) for h in range(2) for k in range(1, nb + 1)]
+    lag = min(3, nb)
     for n, unit in enumerate(order):
         section(*unit)
-        if n > 0:
-            pass_on(*order[n - 1])
-    pass_on(*order[-1])
+        if n >= lag:
+            pass_on(*order[n - lag])
+    for unit in order[-lag:]:
+        pass_on(*unit)
 
     def features(t0):
         rows = t0 * FS

time: 42 us -> 42.9 us (1.021)
  Pallas kernels: 36.4 us -> 37.3 us
    pallas_call x1, Pallas kernels: 36.4 us -> 37.3 us  [per_device(): pl.pallas_call(functools.partial(kernel, cfg), out_shape=(jax.ShapeDtypeS...]
where the time goes in v3:
time: 42.9 us; the launch traced here: 42.7 us
  Pallas kernels  37.3 us (87%)
  local copies, waits for them, and re-layouts  4.7 us (11%)
  between operations  0.65 us (2%)
    pallas_call x1, Pallas kernels, per_device(): pl.pallas_call(functools.partial(kernel, cfg), out_shape=(jax.ShapeDtypeS...  37.3 us
    unnamed x1, local copies, waits for them, and re-layouts  1.75 us
    transpose x1, local copies, waits for them, and re-layouts, per_device(): sp = lax.dynamic_slice(grads, (0, lax.rem(b * rs, 128)), (cw, rs)).T  1.63 us
    transpose x1, local copies, waits for them, and re-layouts, per_device(): lax.dynamic_slice(grads, (0, sp_lanes + lax.rem(b * rt, 128)), (cw, rt))  1.32 us

profile of v3, /device:TPU:0, one launch (start us, length us, event | category | flops | bytes accessed | tf_op | source)
XLA Modules:
  0.0 42.7 jit_solution(9050982538794174486)
XLA Ops:
  0.6 37.3 %shard_map.85 = (bf16[23,32,256]{2,1,0:T(8,128)(2,1)}, f32[32,768]{1,0:T(8,128)}) custom-call(bf16[23,270,256]{2,1,0:T(8,128)(2,1)} %tiles_ref.1, bf16[23,32,256]{2,1,0:T(8,128)(2,1)} %cot_ref.1, s32[3,23]{1,0:T(4,128)} %bitcast.5, s32[1,4,6]{2,1,0:T(4,128)} %plan_ref.1, bf16[576,256]{1,0:T(8,128)(2,1)} %wsp_ref.1, bf16[128,256]{1,0:T(8,128)(2,1)} %wtp_ref.1), custom_call_target="tpu_custom_call" | custom-call | tf_op jit(solution)/shard_map/pallas_call | solution.py:466
  38.0 1.6 %dynamic-slice_bitcast_fusion = f32[576,32]{0,1:T(8,128)} fusion(f32[32,768]{1,0:T(8,128)} %get-tuple-element.6, s32[]{:T(128)S(6)} %select_n.6), kind=kLoop, calls=%fused_computation | loop fusion | bytes 147460 | tf_op jit(solution)/shard_map/transpose | solution.py:480
  39.6 1.3 %dynamic-slice_bitcast_fusion.1 = f32[128,32]{0,1:T(8,128)} fusion(f32[32,768]{1,0:T(8,128)} %get-tuple-element.6, s32[]{:T(128)S(6)} %select_n.7), kind=kLoop, calls=%fused_computation.1 | loop fusion | bytes 32772 | tf_op jit(solution)/shard_map/transpose | solution.py:481
  40.9 1.8 %copy.10 = bf16[23,32,256]{2,1,0:T(8,128)(2,1)} copy(bf16[23,32,256]{2,1,0:T(8,128)(2,1)} %get-tuple-element.10) | data formatting | bytes 753664

commit v4 on v3

--- a/solution.py
+++ b/solution.py
@@ -13,6 +13,7 @@
 WORK_TILES = 12
 F32, BF16 = jnp.float32, jnp.bfloat16
 MESH = pl.DeviceIdType.MESH
+VMEM_LIMIT = 64 * 1024 * 1024 - 65536
 
 
 def up(value, step):
@@ -22,7 +23,7 @@
 def kernel(
     cfg,
     tiles_ref, cot_ref, flags_ref, plan_ref, wsp_ref, wtp_ref,
-    feat_ref, grad_ref,
+    feat_ref, sp_ref, tp_ref,
     cbuf, fbuf, pbuf, ftmp, tbuf, xf, cf, patches, cotp, wsp, wtp, act, dact, grad_t, cot_t, live, masks,
     own, s1, r1, s2, r2, own3, s3, r3,
     tile_sem, loc_sem, ag_send, ag_recv, zr_send, zr_recv, fw_send, fw_recv,
@@ -390,18 +391,40 @@
     lax.fori_loop(0, owned, feat_out, 0)
     feat_copy = local_copy(cbuf, feat_ref, loc_sem.at[5])
     group_sum(1)
+    sums = []
     for h in range(2):
         at = bounds[h]
         total = own3[z, :, at]
         for k in range(1, nz):
             third[h, k].wait_recv()
             total = total + r3[k - 1, :, at].astype(F32)[0:cw]
-        grad_ref[:, at] = total * cfg["factor"]
+        sums.append(total * cfg["factor"])
+    total = jnp.concatenate(sums, axis=1)
+    sp_sum, tp_sum = total[:, :sp_lanes], total[:, sp_lanes:]
+    if rs % 128:
+        sp_sum = pltpu.roll(sp_sum, lax.rem(sp_lanes - lax.rem(b * rs, 128), sp_lanes), 1)
+    if rt % 128:
+        tp_sum = pltpu.roll(tp_sum, lax.rem(128 - lax.rem(b * rt, 128), 128), 1)
+    sp_ref[...] = sp_sum[:, :rs]
+    tp_ref[...] = tp_sum[:, :rt]
 
     feat_copy.wait()
     for group in (gathers, relays, forwards, first, second, third):
         for cp in group.values():
             cp.wait_send()
+
+
+def hand_out(feat_in, sp_in, tp_in, feat_out, sp_out, tp_out, sem):
+    copies = [
+        pltpu.make_async_copy(src, dst, sem.at[n])
+        for n, (src, dst) in enumerate(
+            ((feat_in, feat_out), (sp_in, sp_out), (tp_in, tp_out))
+        )
+    ]
+    for cp in copies:
+        cp.start()
+    for cp in copies:
+        cp.wait()
 
 
 def per_device(tiles, cotangent, halo_flags, send_plan, spatial_weight, temporal_weight):
@@ -463,23 +486,30 @@
         dma((2, nb - 1)), dma((2, nb - 1)),
         dma((2, nz - 1)), dma((2, nz - 1)),
     ]
-    features, grads = pl.pallas_call(
+    shapes = (
+        jax.ShapeDtypeStruct((owned, opix, C), BF16),
+        jax.ShapeDtypeStruct((cw, rs), F32),
+        jax.ShapeDtypeStruct((cw, rt), F32),
+    )
+    results = pl.pallas_call(
         functools.partial(kernel, cfg),
-        out_shape=(
-            jax.ShapeDtypeStruct((owned, opix, C), BF16),
-            jax.ShapeDtypeStruct((cw, nl), F32),
-        ),
+        out_shape=shapes,
         in_specs=[hbm] * 6,
-        out_specs=(hbm, vspec),
+        out_specs=(hbm, vspec, vspec),
         scratch_shapes=scratch,
         compiler_params=pltpu.CompilerParams(
-            collective_id=0, has_side_effects=True, vmem_limit_bytes=64 * 1024 * 1024 - 65536
+            collective_id=0, has_side_effects=True, vmem_limit_bytes=VMEM_LIMIT
         ),
     )(tiles, cotangent, halo_flags.T, send_plan, spatial_weight, temporal_weight)
-    b = lax.axis_index("bal")
-    sp = lax.dynamic_slice(grads, (0, lax.rem(b * rs, 128)), (cw, rs)).T
-    tp = lax.dynamic_slice(grads, (0, sp_lanes + lax.rem(b * rt, 128)), (cw, rt)).T
-    return (features, sp, tp)
+    features, sp, tp = pl.pallas_call(
+        hand_out,
+        out_shape=shapes,
+        in_specs=[hbm] * 3,
+        out_specs=(hbm, hbm, hbm),
+        scratch_shapes=[dma((3,))],
+        compiler_params=pltpu.CompilerParams(vmem_limit_bytes=VMEM_LIMIT),
+    )(*results)
+    return (features, sp.T, tp.T)
 
 
 def solution(mesh):

time: 42.9 us -> 53.7 us (1.25)
  Pallas kernels: 37.3 us -> 53 us
  local copies, waits for them, and re-layouts: 4.7 us -> 0 us
    pallas_call x1 -> x2, Pallas kernels: 37.3 us -> 53 us  [the longest x1 37.4 us: per_device(): pl.pallas_call(functools.partial(kernel, cfg), out_shape=shapes, in_specs...]
    transpose x2 -> x0, local copies, waits for them, and re-layouts: 2.95 us -> none  [the longest x1 1.63 us: per_device(): sp = lax.dynamic_slice(grads, (0, lax.rem(b * rs, 128)), (cw, rs)).T]
    unnamed x1 -> x0, local copies, waits for them, and re-layouts: 1.75 us -> none
where the time goes in v4:
time: 53.7 us; the launch traced here: 53.6 us
  Pallas kernels  53 us (99%)
  between operations  0.64 us (1%)
    pallas_call x1, Pallas kernels, per_device(): pl.pallas_call(functools.partial(kernel, cfg), out_shape=shapes, in_specs...  37.4 us
    pallas_call x1, Pallas kernels, per_device(): pl.pallas_call(hand_out, out_shape=shapes, in_specs=[hbm] * 3, out_specs=...  15.5 us

profile of v4, /device:TPU:0, one launch (start us, length us, event | category | flops | bytes accessed | tf_op | source)
XLA Modules:
  0.0 53.6 jit_solution(13285630122496820468)
XLA Ops:
  0.6 37.4 %shard_map.85 = (bf16[23,32,256]{2,1,0:T(8,128)(2,1)}, f32[32,576]{1,0:T(8,128)}, f32[32,128]{1,0:T(8,128)}) custom-call(bf16[23,270,256]{2,1,0:T(8,128)(2,1)} %tiles_ref.1, bf16[23,32,256]{2,1,0:T(8,128)(2,1)} %cot_ref.1, s32[3,23]{1,0:T(4,128)} %bitcast.3, s32[1,4,6]{2,1,0:T(4,128)} %plan_ref.1, bf16[576,256]{1,0:T(8,128)(2,1)} %wsp_ref.1, ...), custom_call_target="tpu_custom_call" | custom-call | tf_op jit(solution)/shard_map/pallas_call | solution.py:494
  38.1 15.5 %shard_map.86 = (bf16[23,32,256]{2,1,0:T(8,128)(2,1)}, f32[32,576]{1,0:T(8,128)}, f32[32,128]{1,0:T(8,128)}) custom-call(bf16[23,32,256]{2,1,0:T(8,128)(2,1)} %get-tuple-element.9.feat_in, f32[32,576]{1,0:T(8,128)} %get-tuple-element.10.sp_in, f32[32,128]{1,0:T(8,128)} %get-tuple-element.11.tp_in), custom_call_target="tpu_custom_call" | custom-call | tf_op jit(solution)/shard_map/pallas_call | solution.py:504

commit v5 on v4

--- a/solution.py
+++ b/solution.py
@@ -64,6 +64,12 @@
             barrier, inc=1, device_id=(2 * z_peer(k) + core, b), device_id_type=MESH
         )
 
+    my_sp = pl.ds(pl.multiple_of(b * rs, 16), rs)
+    my_tp = pl.ds(pl.multiple_of(b * rt, 16), rt)
+    local = [
+        local_copy(wsp_ref, wsp.at[my_sp], loc_sem.at[0]),
+        local_copy(wtp_ref, wtp.at[my_tp], loc_sem.at[1]),
+    ]
     small_copies = [
         local_copy(flags_ref, fbuf, loc_sem.at[2]),
         local_copy(plan_ref, pbuf, loc_sem.at[3]),
@@ -76,18 +82,13 @@
         cp = local_copy(tiles_ref.at[part], tbuf.at[part], tile_sem.at[n])
         tile_copies.append((cp, lo, count))
         lo += count
-    my_sp = pl.ds(pl.multiple_of(b * rs, 16), rs)
-    my_tp = pl.ds(pl.multiple_of(b * rt, 16), rt)
-    local = [
-        local_copy(wsp_ref, wsp.at[my_sp], loc_sem.at[0]),
-        local_copy(wtp_ref, wtp.at[my_tp], loc_sem.at[1]),
-    ]
-
     if S > owned:
         for h in range(2):
             cf[h, owned * cs : S * cs, :] = jnp.zeros(((S - owned) * cs, 128), F32)
             xf[h, owned * ts : S * ts, :] = jnp.zeros(((S - owned) * ts, 128), F32)
 
+    for cp in local:
+        cp.wait()
     pl.semaphore_wait(barrier, nb + nz - 1)
 
     lanes = pl.ds(pl.multiple_of(core * half, 128), half)
@@ -106,7 +107,7 @@
     for k in range(1, nb):
         for n, (src, dst, size, fetch, rest) in enumerate(weights):
             cp = pltpu.make_async_remote_copy(
-                src_ref=src.at[rows_at(zpar * rest, fetch), lanes],
+                src_ref=dst.at[rows_at(b * size + zpar * rest, fetch), lanes],
                 dst_ref=dst.at[rows_at(b * size + zpar * rest, fetch), lanes],
                 send_sem=ag_send.at[n, k - 1],
                 recv_sem=ag_recv.at[n, k - 1],
@@ -256,8 +257,6 @@
             lax.fori_loop(cuts[n], cuts[n + 1], patch_rows, 0)
     for k in range(max(steps - 1, 1), nb):
         relay_rest(k)
-    for cp in local:
-        cp.wait()
     for cp in forwards.values():
         cp.wait_recv()
 
@@ -414,16 +413,18 @@
             cp.wait_send()
 
 
-def hand_out(feat_in, sp_in, tp_in, feat_out, sp_out, tp_out, sem):
-    copies = [
-        pltpu.make_async_copy(src, dst, sem.at[n])
-        for n, (src, dst) in enumerate(
-            ((feat_in, feat_out), (sp_in, sp_out), (tp_in, tp_out))
-        )
-    ]
-    for cp in copies:
+def hand_out(feat_in, sp_in, tp_in, feat_out, sp_out, tp_out, feat_buf, sp_buf, tp_buf, sem):
+    ways = (
+        (feat_in, feat_buf, feat_out), (sp_in, sp_buf, sp_out), (tp_in, tp_buf, tp_out)
+    )
+    loads = [pltpu.make_async_copy(w[0], w[1], sem.at[0, n]) for n, w in enumerate(ways)]
+    stores = [pltpu.make_async_copy(w[1], w[2], sem.at[1, n]) for n, w in enumerate(ways)]
+    for cp in loads:
         cp.start()
-    for cp in copies:
+    for load, store in zip(loads, stores):
+        load.wait()
+        store.start()
+    for cp in stores:
         cp.wait()
 
 
@@ -506,7 +507,7 @@
         out_shape=shapes,
         in_specs=[hbm] * 3,
         out_specs=(hbm, hbm, hbm),
-        scratch_shapes=[dma((3,))],
+        scratch_shapes=[vm(x.shape, x.dtype) for x in shapes] + [dma((2, 3))],
         compiler_params=pltpu.CompilerParams(vmem_limit_bytes=VMEM_LIMIT),
     )(*results)
     return (features, sp.T, tp.T)

time: 53.7 us -> 39.8 us (0.74)
  Pallas kernels: 53 us -> 39 us
    pallas_call x1, Pallas kernels: 15.5 us -> 1.8 us  [per_device(): pl.pallas_call(hand_out, out_shape=shapes, in_specs=[hbm] * 3, out_specs=...]
where the time goes in v5:
time: 39.8 us; the launch traced here: 39.7 us
  Pallas kernels  39 us (98%)
  between operations  0.64 us (2%)
    pallas_call x1, Pallas kernels, per_device(): pl.pallas_call(functools.partial(kernel, cfg), out_shape=shapes, in_specs...  37.2 us
    pallas_call x1, Pallas kernels, per_device(): pl.pallas_call(hand_out, out_shape=shapes, in_specs=[hbm] * 3, out_specs=...  1.8 us

profile of v5, /device:TPU:0, one launch (start us, length us, event | category | flops | bytes accessed | tf_op | source)
XLA Modules:
  0.0 39.7 jit_solution(17558047352383899610)
XLA Ops:
  0.6 37.2 %shard_map.85 = (bf16[23,32,256]{2,1,0:T(8,128)(2,1)}, f32[32,576]{1,0:T(8,128)}, f32[32,128]{1,0:T(8,128)}) custom-call(bf16[23,270,256]{2,1,0:T(8,128)(2,1)} %tiles_ref.1, bf16[23,32,256]{2,1,0:T(8,128)(2,1)} %cot_ref.1, s32[3,23]{1,0:T(4,128)} %bitcast.3, s32[1,4,6]{2,1,0:T(4,128)} %plan_ref.1, bf16[576,256]{1,0:T(8,128)(2,1)} %wsp_ref.1, ...), custom_call_target="tpu_custom_call" | custom-call | tf_op jit(solution)/shard_map/pallas_call | solution.py:495
  37.9 1.8 %shard_map.86 = (bf16[23,32,256]{2,1,0:T(8,128)(2,1)}, f32[32,576]{1,0:T(8,128)}, f32[32,128]{1,0:T(8,128)}) custom-call(bf16[23,32,256]{2,1,0:T(8,128)(2,1)} %get-tuple-element.9.feat_in, f32[32,576]{1,0:T(8,128)} %get-tuple-element.10.sp_in, f32[32,128]{1,0:T(8,128)} %get-tuple-element.11.tp_in), custom_call_target="tpu_custom_call" | custom-call | tf_op jit(solution)/shard_map/pallas_call | solution.py:505

commit v6 on v5

--- a/solution.py
+++ b/solution.py
@@ -206,7 +206,7 @@
 
     for n in range(2):
         rows = n * 2 * FS
-        store_split(cot_t, cotp[rows : rows + 2 * FS, :].astype(F32).T, rows, 2 * FS)
+        store_split(cot_t, cotp[rows : rows + 2 * FS, :].astype(BF16 if cw % 16 == 0 else F32).T, rows, 2 * FS)
 
     def tile_in(s, carry):
         v = tbuf[s].astype(F32)
@@ -279,7 +279,7 @@
             )
             ga = g if ga is None else ga + g
         gp = ga * (sig * (1.0 + pre * (1.0 - sig)))
-        store_split(grad_t, gp.T, rows, 2 * FS)
+        store_split(grad_t, (gp.astype(BF16) if cw % 16 == 0 else gp).T, rows, 2 * FS)
 
     for n in range(3):
         chunk(n)
@@ -378,8 +378,8 @@
             third[h, k] = cp
 
     features(0)
+    group_sum(0)
     features(2)
-    group_sum(0)
 
     def feat_out(s, carry):
         cbuf[s] = jnp.concatenate(

time: 39.8 us -> 39.8 us (level)
  no operation moved by 1% of the time
where the time goes in v6:
time: 39.8 us; the launch traced here: 39.7 us
  Pallas kernels  39 us (98%)
  between operations  0.64 us (2%)
    pallas_call x1, Pallas kernels, per_device(): pl.pallas_call(functools.partial(kernel, cfg), out_shape=shapes, in_specs...  37.2 us
    pallas_call x1, Pallas kernels, per_device(): pl.pallas_call(hand_out, out_shape=shapes, in_specs=[hbm] * 3, out_specs=...  1.8 us

profile of v6, /device:TPU:0, one launch (start us, length us, event | category | flops | bytes accessed | tf_op | source)
XLA Modules:
  0.0 39.7 jit_solution(5150492665382910242)
XLA Ops:
  0.6 37.2 %shard_map.85 = (bf16[23,32,256]{2,1,0:T(8,128)(2,1)}, f32[32,576]{1,0:T(8,128)}, f32[32,128]{1,0:T(8,128)}) custom-call(bf16[23,270,256]{2,1,0:T(8,128)(2,1)} %tiles_ref.1, bf16[23,32,256]{2,1,0:T(8,128)(2,1)} %cot_ref.1, s32[3,23]{1,0:T(4,128)} %bitcast.3, s32[1,4,6]{2,1,0:T(4,128)} %plan_ref.1, bf16[576,256]{1,0:T(8,128)(2,1)} %wsp_ref.1, ...), custom_call_target="tpu_custom_call" | custom-call | tf_op jit(solution)/shard_map/pallas_call | solution.py:495
  37.9 1.8 %shard_map.86 = (bf16[23,32,256]{2,1,0:T(8,128)(2,1)}, f32[32,576]{1,0:T(8,128)}, f32[32,128]{1,0:T(8,128)}) custom-call(bf16[23,32,256]{2,1,0:T(8,128)(2,1)} %get-tuple-element.9.feat_in, f32[32,576]{1,0:T(8,128)} %get-tuple-element.10.sp_in, f32[32,128]{1,0:T(8,128)} %get-tuple-element.11.tp_in), custom_call_target="tpu_custom_call" | custom-call | tf_op jit(solution)/shard_map/pallas_call | solution.py:505
